TPU v7x, 32 devices: a whole 2x2x4 slice. The times are simulated.
32 devices in a mesh: groups: 2 (over x), dap: 16 (over z, y, core).
Axes of the slice: x: 2, y: 2, z: 4, core: 2. Of those that a mesh axis runs over, the one named last changes fastest.
Arguments:
- pair_state: bfloat16 [128, 64, 128], P(('groups', 'dap')), parts along dimension 0, may hold values from -200 to 200
- cotangent: bfloat16 [128, 64, 128], P(('groups', 'dap')), parts along dimension 0, may hold values from -6 to 6
- pair_mask: int32 [128, 64], P(('groups', 'dap')), parts along dimension 0, may hold values 0 or 1
- token_count: int32 [2], P('groups'), parts along dimension 0, may hold values from 32 to 64
- norm_gain: float32 [128], replicated, may hold values from 0.1 to 1.9
- norm_shift: float32 [128], replicated, may hold values from -3 to 3
- w_edges: bfloat16 [128, 256], replicated, may hold values from -0.5 to 0.5
- w_gate: bfloat16 [128, 128], replicated, may hold values from -0.5 to 0.5
- edge_gain: float32 [64], replicated, may hold values from 0.1 to 1.9
- edge_shift: float32 [64], replicated, may hold values from -3 to 3
- w_out: bfloat16 [64, 128], replicated, may hold values from -0.75 to 0.75
- final_gain: float32 [128], replicated, may hold values from 0.1 to 1.9
- final_shift: float32 [128], replicated, may hold values from -3 to 3
- w_expand: bfloat16 [128, 1024], replicated, may hold values from -0.5 to 0.5
- w_contract: bfloat16 [512, 128], replicated, may hold values from -0.25 to 0.25
Outputs:
- grad_pair: bfloat16 [128, 64, 128], P(('groups', 'dap')), parts along dimension 0
- norm_grads: float32 [8, 128], P('groups'), parts along dimension 0
- edge_grads: float32 [4, 64], P('groups'), parts along dimension 0
There are 2 independent parts, one for each index of `groups`. A program takes and returns all parts, laid end to end along the dimension named above; an argument that names none is the same for every part. Nothing has to cross between parts.
All inputs are finite; a program needn't handle non-finite values. No bound on the sum of `pair_mask` on one device may be relied on, other than what follows from the above.
Results may differ from a plain program's by a relative error of at most 0.012.
Values may be sent and summed in bfloat16 or wider, within the bound.
A program may use at most 192 MiB of HBM per device.

v0:
```python
import jax
import jax.numpy as jnp
from jax import lax
from jax.sharding import PartitionSpec as P

epsilon = 1e-05
block_cols = 64


def layer_norm(values, norm_scale, norm_offset):
    centre = jnp.mean(values, axis=-1, keepdims=True)
    centred = values - centre
    spread = jnp.mean(centred * centred, axis=-1, keepdims=True)
    return centred * lax.rsqrt(spread + epsilon) * norm_scale + norm_offset


def project_edges(state, validity, scale_in, offset_in, w_edges, w_gate):
    normed = layer_norm(state.astype(jnp.float32), scale_in, offset_in).astype(jnp.bfloat16)
    channels = w_edges.shape[1] // 4
    mixed = jnp.dot(normed, w_edges, preferred_element_type=jnp.float32)
    weight_mask = validity[..., None]
    left_edges = (
        jax.nn.sigmoid(mixed[..., :channels]) * mixed[..., channels : 2 * channels] * weight_mask
    )
    right_edges = (
        jax.nn.sigmoid(mixed[..., 2 * channels : 3 * channels])
        * mixed[..., 3 * channels :]
        * weight_mask
    )
    gating = jax.nn.sigmoid(jnp.dot(normed, w_gate, preferred_element_type=jnp.float32))
    return (
        left_edges.astype(jnp.bfloat16),
        right_edges.astype(jnp.bfloat16),
        gating.astype(jnp.bfloat16),
    )


def finish_block(
    state,
    edges,
    gating,
    edge_scale,
    edge_offset,
    final_scale,
    final_offset,
    w_out,
    w_expand,
    w_contract,
):
    edge_normed = layer_norm(edges, edge_scale, edge_offset).astype(jnp.bfloat16)
    update = gating.astype(jnp.float32) * jnp.dot(
        edge_normed, w_out, preferred_element_type=jnp.float32
    )
    middle = (state.astype(jnp.float32) + update).astype(jnp.bfloat16).astype(jnp.float32)
    normed = layer_norm(middle, final_scale, final_offset).astype(jnp.bfloat16)
    expanded = jnp.dot(normed, w_expand, preferred_element_type=jnp.float32)
    hidden_units = w_contract.shape[0]
    activated = (jax.nn.silu(expanded[..., :hidden_units]) * expanded[..., hidden_units:]).astype(
        jnp.bfloat16
    )
    return middle + jnp.dot(activated, w_contract, preferred_element_type=jnp.float32)


def body(
    pair_state,
    cotangent,
    pair_mask,
    token_count,
    norm_gain,
    norm_shift,
    w_edges,
    w_gate,
    edge_gain,
    edge_shift,
    w_out,
    final_gain,
    final_shift,
    w_expand,
    w_contract,
):
    rows_dev = pair_state.shape[0]
    tokens_all = pair_state.shape[1]
    first_row = lax.axis_index("dap") * rows_dev
    row_ids = first_row + jnp.arange(rows_dev, dtype=jnp.int32)
    column_ids = jnp.arange(tokens_all, dtype=jnp.int32)
    live_count = token_count[0]
    validity = (
        pair_mask.astype(jnp.float32)
        * (row_ids < live_count).astype(jnp.float32)[:, None]
        * (column_ids < live_count).astype(jnp.float32)[None, :]
    )

    def project_local(state_in, scale_in, offset_in):
        return project_edges(state_in, validity, scale_in, offset_in, w_edges, w_gate)

    outputs, project_back = jax.vjp(project_local, pair_state, norm_gain, norm_shift)
    left_edges, right_edges, gating = lax.optimization_barrier(outputs)
    left_rows = left_edges.transpose(2, 0, 1)
    right_rows = right_edges.transpose(2, 0, 1)
    channels = left_rows.shape[0]

    def finish_local(state_in, edges_in, gate_in, scale_a, offset_a, scale_b, offset_b):
        return finish_block(
            state_in,
            edges_in,
            gate_in,
            scale_a,
            offset_a,
            scale_b,
            offset_b,
            w_out,
            w_expand,
            w_contract,
        )

    def absorb_block(carry_in, piece_rows, offset_at):
        left_grad, edge_grads_all, state_grad, gate_grad, norm_sums = carry_in
        width_now = piece_rows.shape[1]
        edges = jnp.einsum(
            "cik,cjk->cij", left_rows, piece_rows, preferred_element_type=jnp.float32
        )
        state_part = lax.dynamic_slice_in_dim(pair_state, offset_at, width_now, 1)
        gate_part = lax.dynamic_slice_in_dim(gating, offset_at, width_now, 1)
        cotan_part = lax.dynamic_slice_in_dim(cotangent, offset_at, width_now, 1)
        _, finish_back = jax.vjp(
            finish_local,
            state_part,
            edges.transpose(1, 2, 0),
            gate_part,
            edge_gain,
            edge_shift,
            final_gain,
            final_shift,
        )
        grads = finish_back(cotan_part.astype(jnp.float32))
        edge_round = grads[1].transpose(2, 0, 1).astype(jnp.bfloat16)
        left_grad = left_grad + jnp.einsum(
            "cij,cjk->cik", edge_round, piece_rows, preferred_element_type=jnp.float32
        )
        edge_grads_all = lax.dynamic_update_slice_in_dim(edge_grads_all, edge_round, offset_at, 2)
        state_grad = lax.dynamic_update_slice_in_dim(state_grad, grads[0], offset_at, 1)
        gate_grad = lax.dynamic_update_slice_in_dim(gate_grad, grads[2], offset_at, 1)
        norm_sums = (
            norm_sums[0] + grads[3],
            norm_sums[1] + grads[4],
            norm_sums[2] + grads[5],
            norm_sums[3] + grads[6],
        )
        return (left_grad, edge_grads_all, state_grad, gate_grad, norm_sums)

    def absorb(carry_in, piece_rows, offset_at):
        width_now = piece_rows.shape[1]
        if width_now > block_cols and width_now % block_cols == 0:

            def step_block(index_at, carry_now):
                begin = index_at * block_cols
                part_rows = lax.dynamic_slice_in_dim(piece_rows, begin, block_cols, 1)
                return absorb_block(carry_now, part_rows, offset_at + begin)

            return lax.fori_loop(0, width_now // block_cols, step_block, carry_in)
        return absorb_block(carry_in, piece_rows, offset_at)

    start_carry = (
        jnp.zeros((channels, rows_dev, tokens_all), jnp.float32),
        jnp.zeros((channels, rows_dev, tokens_all), jnp.bfloat16),
        jnp.zeros(pair_state.shape, jnp.bfloat16),
        jnp.zeros(gating.shape, jnp.bfloat16),
        (
            jnp.zeros(edge_gain.shape, jnp.float32),
            jnp.zeros(edge_shift.shape, jnp.float32),
            jnp.zeros(final_gain.shape, jnp.float32),
            jnp.zeros(final_shift.shape, jnp.float32),
        ),
    )
    left_sum, edge_grads_all, late_grad, gate_grad, norm_sums = absorb(
        start_carry, lax.all_gather(right_rows, "dap", axis=1, tiled=True), jnp.int32(0)
    )
    left_grad = left_sum.astype(jnp.bfloat16)
    columns = lax.all_to_all(edge_grads_all, "dap", split_axis=2, concat_axis=1, tiled=True)
    piece_rows = lax.all_gather(left_rows, "dap", axis=1, tiled=True)
    width_now = piece_rows.shape[1]
    right_sum = jnp.einsum("cij,cik->cjk", columns, piece_rows, preferred_element_type=jnp.float32)
    right_grad = right_sum.astype(jnp.bfloat16)
    cotangents = lax.optimization_barrier(
        (left_grad.transpose(1, 2, 0), right_grad.transpose(1, 2, 0), gate_grad)
    )
    early_grad, gain_grad, shift_grad = project_back(cotangents)
    summed = lax.optimization_barrier((early_grad, late_grad))
    grad_pair = (summed[0].astype(jnp.float32) + summed[1].astype(jnp.float32)).astype(jnp.bfloat16)
    pair_terms = jnp.stack([gain_grad, shift_grad, norm_sums[2], norm_sums[3]])
    edge_terms = jnp.stack([norm_sums[0], norm_sums[1]])
    pair_totals, edge_totals = lax.psum((pair_terms, edge_terms), "dap")
    return (grad_pair, pair_totals / tokens_all, edge_totals / tokens_all)


def solution(mesh):
    in_specs = (
        P(("groups", "dap"), None, None),
        P(("groups", "dap"), None, None),
        P(("groups", "dap"), None),
        P("groups"),
        P(),
        P(),
        P(),
        P(),
        P(),
        P(),
        P(),
        P(),
        P(),
        P(),
        P(),
    )
    out_specs = (P(("groups", "dap"), None, None), P("groups", None), P("groups", None))
    return jax.shard_map(body, mesh=mesh, in_specs=in_specs, out_specs=out_specs, check_vma=False)
```

profile of v0, /device:TPU:0, one launch (start us, length us, event | category | flops | bytes accessed | tf_op | source)
XLA Modules:
  0.0 102.9 jit_solution(6378240066876652007)
XLA Ops:
  0.6 0.0 copy-start
  0.7 1.0 convert_reduce_fusion.1
  1.7 0.2 fusion.54
  2.6 0.0 copy-start.8
  2.6 0.0 copy-start.10
  2.6 0.6 copy-done.8
  3.2 0.0 copy-done.10
  3.2 0.3 fusion.77
  3.5 0.5 copy-done.5
  4.0 0.3 fusion.101
  4.3 0.0 copy-start.9
  4.3 0.7 copy-done.9
  5.0 0.1 multiply_multiply_fusion.4
  5.0 0.2 multiply_convert_fusion
  5.2 0.1 copy.53
  5.3 0.1 copy.52
  5.4 26.2 %all_gather.6 = bf16[64,64,64]{2,0,1:T(8,128)(2,1)S(1)} all-gather(bf16[64,4,64]{2,0,1:T(8,128)(2,1)S(1)} %copy.52), channel_id=1, replica_groups=mesh['groups'=2,'dap'=16] {'dap'}, dimensions={1}, use_global_device_ids=true | all-gather | bytes 557056 | tf_op jit(solution)/shard_map/all_gather | solution.py:176
  31.7 0.8 bitcast_reduce_fusion
  32.5 0.1 multiply_reduce_fusion
  32.6 0.0 copy-start.11
  32.6 0.6 copy-done.7
  33.2 0.0 copy-done.11
  33.2 0.2 add_convert_fusion.3
  33.4 0.5 copy-done.4
  34.0 0.3 convert_reduce_fusion.2
  34.3 0.2 fusion.50
  34.5 0.0 copy-start.6
  34.5 0.0 copy-start.12
  34.5 0.6 copy-done.6
  35.1 0.0 copy-done.12
  35.1 0.3 fusion.19
  35.5 0.5 copy-done.3
  36.0 0.1 copy-done.13
  36.1 0.4 multiply_multiply_fusion
  36.5 0.4 fusion.51
  36.9 0.3 fusion.49
  37.1 0.2 fusion.53
  37.3 0.1 fusion.52
  37.5 0.1 copy.56
  37.6 0.1 fusion.43
  37.8 0.7 fusion.57
  38.5 0.1 fusion.59
  38.6 0.1 copy.59
  38.8 0.7 reshape.125
  39.5 3.5 %all-to-all-start = ((bf16[16,2,512]{2,1,0:T(2,128)(2,1)}), bf16[16,2,512]{2,1,0:T(2,128)(2,1)S(1)}, u32[]{:S(2)}, u32[]{:S(2)}) async-start(bf16[16,2,512]{2,1,0:T(2,128)(2,1)} %reshape.125), calls=%async_computation | async-start | bytes 65536 | tf_op jit(solution)/shard_map/all_to_all | solution.py:179
  43.0 0.8 fusion.12
  43.8 0.1 copy.62
  43.9 0.1 copy.58
  44.0 24.7 %all_gather.7 = bf16[64,64,64]{2,0,1:T(8,128)(2,1)S(1)} all-gather(bf16[64,4,64]{2,0,1:T(8,128)(2,1)S(1)} %copy.62), channel_id=1, replica_groups=mesh['groups'=2,'dap'=16] {'dap'}, dimensions={1}, use_global_device_ids=true | all-gather | bytes 557056 | tf_op jit(solution)/shard_map/all_gather | solution.py:180
  68.7 0.0 all-to-all-done
  68.7 0.1 reshape.126
  68.9 0.1 copy.61
  68.9 0.1 copy.63
  69.0 0.8 fusion.7
  69.8 0.1 copy.65
  70.0 0.2 fusion.73
  70.1 0.3 convolution_convert_fusion.2
  70.4 0.3 fusion.55
  70.7 0.3 fusion.46
  71.0 0.2 add_convert_fusion.1
  71.2 29.8 %all-reduce.6 = (f32[4,128]{1,0:T(4,128)S(1)}, f32[2,64]{1,0:T(2,128)S(1)}) all-reduce(f32[4,128]{1,0:T(4,128)S(1)} %pad_maximum_fusion, f32[2,64]{1,0:T(2,128)S(1)} %pad_maximum_fusion.1), channel_id=1, replica_groups=mesh['groups'=2,'dap'=16] {'dap'}, use_global_device_ids=true, to_apply=%region_16.17 | all-reduce | flops 640 | bytes 5120 | tf_op jit(solution)/shard_map/psum | solution.py:192
  101.1 0.6 broadcast_multiply_fusion
  101.6 0.6 broadcast_multiply_fusion.4
  102.2 0.6 add_convert_fusion
  (27 shorter events, 0.1 us)
Async XLA Ops:
  0.6 33.9 %copy-start = (bf16[128,1024]{1,0:T(8,128)(2,1)S(1)}, bf16[128,1024]{1,0:T(8,128)(2,1)}, u32[]{:S(2)}) copy-start(bf16[128,1024]{1,0:T(8,128)(2,1)} %param.28) | copy-start | bytes 786436
  0.6 1.0 %copy-start.1 = (bf16[4,64,128]{2,1,0:T(8,128)(2,1)S(1)}, bf16[4,64,128]{2,1,0:T(8,128)(2,1)}, u32[]{:S(2)}) copy-start(bf16[4,64,128]{2,1,0:T(8,128)(2,1)} %param.15) | copy-start | bytes 196612
  0.7 1.9 %copy-start.2 = (bf16[128,256]{1,0:T(8,128)(2,1)S(1)}, bf16[128,256]{1,0:T(8,128)(2,1)}, u32[]{:S(2)}) copy-start(bf16[128,256]{1,0:T(8,128)(2,1)} %param.21) | copy-start | bytes 196612
  2.6 0.7 copy-start.8
  2.6 0.7 copy-start.10
  3.2 0.8 copy-start.5
  4.3 0.7 copy-start.9
  32.6 0.7 copy-start.7
  32.6 0.7 copy-start.11
  33.2 0.7 copy-start.4
  34.5 0.7 copy-start.6
  34.5 0.7 copy-start.12
  35.1 0.8 copy-start.3
  35.1 0.9 copy-start.13
  39.5 29.2 %all-to-all-start = ((bf16[16,2,512]{2,1,0:T(2,128)(2,1)}), bf16[16,2,512]{2,1,0:T(2,128)(2,1)S(1)}, u32[]{:S(2)}, u32[]{:S(2)}) async-start(bf16[16,2,512]{2,1,0:T(2,128)(2,1)} %reshape.125), calls=%async_computation | async-start | bytes 65536 | tf_op jit(solution)/shard_map/all_to_all | solution.py:179
where the time goes:
time: 103 us
  blocking collectives  80.8 us (78%)
  local copies, waits for them, and re-layouts  6.01 us (6%)
  other arithmetic  5.89 us (6%)
  matrix products  5 us (5%)
  starting transfers between devices  3.5 us (3%)
  between operations  1.66 us (2%)
    psum x1, blocking collectives, body(): pair_totals, edge_totals = lax.psum((pair_terms, edge_terms), 'dap')  29.8 us
    all_gather x1, blocking collectives, body(): lax.all_gather(right_rows, 'dap', axis=1, tiled=True)  26.2 us
    all_gather x1, blocking collectives, body(): piece_rows = lax.all_gather(left_rows, 'dap', axis=1, tiled=True)  24.7 us
    unnamed x30, local copies, waits for them, and re-layouts  5.06 us
    all_to_all x1, starting transfers between devices, body(): lax.all_to_all(edge_grads_all, 'dap', split_axis=2, concat_axis=1, tiled=...  3.5 us
  transfers between devices with their start and end apart: 1, of which 0 were waited for; matrix products, arithmetic and copies ran while one was open for 1% of the time, Pallas kernels for 0%

commit v1 on v0

--- a/solution.py
+++ b/solution.py
@@ -1,6 +1,10 @@
+import functools
+
 import jax
 import jax.numpy as jnp
 from jax import lax
+from jax.experimental import pallas as pl
+from jax.experimental.pallas import tpu as pltpu
 from jax.sharding import PartitionSpec as P
 
 epsilon = 1e-05
@@ -192,6 +196,406 @@
     pair_totals, edge_totals = lax.psum((pair_terms, edge_terms), "dap")
     return (grad_pair, pair_totals / tokens_all, edge_totals / tokens_all)
 
+nn_dims = (((1,), (0,)), ((), ()))
+nt_dims = (((1,), (1,)), ((), ()))
+tn_dims = (((0,), (0,)), ((), ()))
+f32 = jnp.float32
+bf16 = jnp.bfloat16
+
+
+def mul(a, b, dims):
+    return lax.dot_general(a, b, dims, preferred_element_type=f32)
+
+
+def sigmoid(x):
+    return 0.5 * jnp.tanh(0.5 * x) + 0.5
+
+
+def iota(shape, axis):
+    return lax.broadcasted_iota(jnp.int32, shape, axis)
+
+
+def low_half(rows):
+    return iota((rows, 128), 1) < 64
+
+
+def pack(x):
+    low, high = x[:32], x[32:]
+    first = low_half(32)
+    pieces = []
+    for half in range(2):
+        a, b = low[:, half * 128 : half * 128 + 128], high[:, half * 128 : half * 128 + 128]
+        pieces.append(jnp.where(first, a, pltpu.roll(b, 64, 1)))
+        pieces.append(jnp.where(first, pltpu.roll(a, 64, 1), b))
+    return jnp.concatenate(pieces, axis=0)
+
+
+def unpack(x):
+    first = low_half(32)
+    lows, highs = [], []
+    for half in range(2):
+        a, b = x[half * 64 : half * 64 + 32], x[half * 64 + 32 : half * 64 + 64]
+        lows.append(jnp.where(first, a, pltpu.roll(b, 64, 1)))
+        highs.append(jnp.where(first, pltpu.roll(a, 64, 1), b))
+    return jnp.concatenate(
+        [jnp.concatenate(lows, axis=1), jnp.concatenate(highs, axis=1)], axis=0
+    )
+
+
+def one_hot(hit):
+    return jnp.where(hit, 1.0, 0.0).astype(bf16)
+
+
+def channel_sum(x):
+    total = jnp.sum(x, axis=0)
+    total = total + pltpu.roll(total, 4, 0)
+    return total + pltpu.roll(total, 64, 1)
+
+
+def fused_kernel(
+    n,
+    count_ref,
+    state_ref,
+    cot_ref,
+    mask_ref,
+    gain1_ref,
+    shift1_ref,
+    we_ref,
+    wg_ref,
+    gain_e_ref,
+    shift_e_ref,
+    wo_ref,
+    gain2_ref,
+    shift2_ref,
+    wx_ref,
+    wc_ref,
+    out_ref,
+    norm_ref,
+    edge_ref,
+    s1,
+    r1,
+    s2,
+    r2,
+    s3,
+    r3,
+    s4,
+    r4,
+    s5,
+    r5,
+    dact_ref,
+    send_sem,
+    recv_sem,
+):
+    me = lax.axis_index("dap")
+    group = lax.axis_index("groups")
+    cells = state_ref.shape[0] * state_ref.shape[1]
+    tokens = state_ref.shape[1]
+
+    barrier = pltpu.get_barrier_semaphore()
+
+    def greet(step, carry):
+        peer = lax.rem(me + step, n)
+        pl.semaphore_signal(
+            barrier, inc=1, device_id=(group, peer), device_id_type=pl.DeviceIdType.MESH
+        )
+        return carry
+
+    lax.fori_loop(1, n, greet, 0)
+
+    def scatter(phase, src, dst, same):
+        def send(step, carry):
+            peer = lax.rem(me + step, n)
+            pltpu.make_async_remote_copy(
+                src_ref=src if same else src.at[peer],
+                dst_ref=dst.at[me],
+                send_sem=send_sem.at[phase],
+                recv_sem=recv_sem.at[phase],
+                device_id=(group, peer),
+                device_id_type=pl.DeviceIdType.MESH,
+            ).start()
+            return carry
+
+        lax.fori_loop(1, n, send, 0)
+
+    def arrive(phase, dst):
+        part = dst.at[pl.ds(0, n - 1)]
+        pltpu.make_async_copy(part, part, recv_sem.at[phase]).wait()
+
+    def sent(phase, dst):
+        part = dst.at[pl.ds(0, n - 1)]
+        pltpu.make_async_copy(part, part, send_sem.at[phase]).wait()
+
+    state = state_ref[...].reshape(cells, 128).astype(f32)
+    gain1 = gain1_ref[...]
+    centred = state - jnp.mean(state, axis=1, keepdims=True)
+    rstd1 = lax.rsqrt(jnp.mean(centred * centred, axis=1, keepdims=True) + epsilon)
+    hat1 = centred * rstd1
+    normed = (hat1 * gain1 + shift1_ref[...]).astype(bf16)
+    we_t = we_ref[...].T
+    mixed = mul(we_t, normed, nt_dims)
+    count = count_ref[0]
+    mask = mask_ref[...].astype(f32)
+    mask = jnp.concatenate([mask[i : i + 1] for i in range(4)], axis=1)
+    cell = iota((1, cells), 1)
+    live = (cell % tokens < count) & (me * 4 + cell // tokens < count)
+    valid = jnp.where(live, mask, 0.0)
+    sig_l, val_l = sigmoid(mixed[:64]), mixed[64:128]
+    sig_r, val_r = sigmoid(mixed[128:192]), mixed[192:]
+    left = pack(sig_l * val_l * valid).astype(bf16)
+    right = pack(sig_r * val_r * valid).astype(bf16)
+    row, col = iota((128, 128), 0), iota((128, 128), 1)
+    to_owner = one_hot(col == (row % 4) * 32 + (row // 8) * 2 + (row // 4) % 2)
+    from_owner = one_hot(row == (col % 4) * 32 + (col // 8) * 2 + (col // 4) % 2)
+    both = mul(to_owner, jnp.concatenate([left, right], axis=1), nn_dims)
+    both = jnp.concatenate(
+        [both[:, :128].reshape(n, 8, 128), both[:, 128:].reshape(n, 8, 128)], axis=1
+    ).astype(bf16)
+    s1[...] = both
+    r1[me] = s1[me]
+    pl.semaphore_wait(barrier, n - 1)
+    scatter(0, s1, r1, False)
+
+    gating = sigmoid(mul(normed, wg_ref[...], nn_dims)).astype(bf16).astype(f32)
+    cot = cot_ref[...].reshape(cells, 128)
+    dact_ref[...] = mul(cot, wc_ref[...], nt_dims).astype(bf16)
+    lane64 = iota((128, 64), 1)
+    row64 = iota((128, 64), 0) // 4
+    first = low_half(128)
+
+    def spread(vector):
+        low = jnp.sum(jnp.where(lane64 == row64, vector, 0.0), axis=1, keepdims=True)
+        high = jnp.sum(jnp.where(lane64 == row64 + 32, vector, 0.0), axis=1, keepdims=True)
+        return jnp.where(first, low, high).reshape(n, 8, 128)
+
+    gain_e, shift_e = spread(gain_e_ref[...]), spread(shift_e_ref[...])
+    by_pair = one_hot(col == ((row % 64) // 4) * 8 + (row // 64) * 4 + row % 4)
+    pair_rows = one_hot(row == ((col % 64) // 4) * 8 + (col // 64) * 4 + col % 4)
+    even = (iota((128, 128), 0) // 4) % 2 == 0
+
+    arrive(0, r1)
+    got = r1[...].astype(f32)
+    left_all = got[:, :8].reshape(128, 128)
+    right_all = mul(by_pair, got[:, 8:].reshape(128, 128).astype(bf16), nn_dims)
+    first64 = low_half(64)
+
+    def diagonal(x):
+        return jnp.concatenate([jnp.where(first64, x, 0.0), jnp.where(first64, 0.0, x)], axis=0)
+
+    diag0 = diagonal(right_all[:64]).astype(bf16)
+    diag1 = diagonal(right_all[64:]).astype(bf16)
+
+    def by_parity(x):
+        return jnp.where(even, x, 0.0).astype(bf16), jnp.where(even, 0.0, x).astype(bf16)
+
+    left0, left1 = by_parity(left_all)
+    edges = mul(left0, diag0, nt_dims) + mul(left1, diag1, nt_dims)
+    s2[...] = edges.reshape(n, 8, 128)
+    r2[me] = s2[me]
+    scatter(1, s2, r2, False)
+    left_bf = left_all.astype(bf16)
+    arrive(1, r2)
+
+    edges_in = r2[...]
+    inv_c = 1.0 / 64
+    centred_e = edges_in - channel_sum(edges_in) * inv_c
+    rstd_e = lax.rsqrt(channel_sum(centred_e * centred_e) * inv_c + epsilon)
+    hat_e = centred_e * rstd_e
+    edge_normed = (hat_e * gain_e + shift_e).reshape(128, 128).astype(bf16)
+    edge_normed = unpack(mul(from_owner, edge_normed, nn_dims)).astype(bf16)
+    update = mul(edge_normed, wo_ref[...], tn_dims)
+    middle = (state + gating * update).astype(bf16).astype(f32)
+    centred2 = middle - jnp.mean(middle, axis=1, keepdims=True)
+    rstd2 = lax.rsqrt(jnp.mean(centred2 * centred2, axis=1, keepdims=True) + epsilon)
+    hat2 = centred2 * rstd2
+    gain2 = gain2_ref[...]
+    normed2 = (hat2 * gain2 + shift2_ref[...]).astype(bf16)
+    units = wc_ref.shape[0]
+    dnormed2 = jnp.zeros((cells, 128), f32)
+    for begin in range(0, units, 256):
+        w_swish = wx_ref[:, begin : begin + 256]
+        w_linear = wx_ref[:, units + begin : units + begin + 256]
+        swish_in = mul(normed2, w_swish, nn_dims)
+        linear = mul(normed2, w_linear, nn_dims)
+        dact = dact_ref[:, begin : begin + 256].astype(f32)
+        sig = sigmoid(swish_in)
+        silu = swish_in * sig
+        dlinear = (dact * silu).astype(bf16)
+        dswish = (dact * linear * (sig + silu * (1.0 - sig))).astype(bf16)
+        dnormed2 = dnormed2 + mul(dswish, w_swish, nt_dims) + mul(dlinear, w_linear, nt_dims)
+    dnormed2 = dnormed2.astype(bf16).astype(f32)
+    dhat2 = dnormed2 * gain2
+    dmiddle = rstd2 * (
+        dhat2
+        - jnp.mean(dhat2, axis=1, keepdims=True)
+        - hat2 * jnp.mean(dhat2 * hat2, axis=1, keepdims=True)
+    )
+    late = (cot.astype(f32) + dmiddle).astype(bf16).astype(f32)
+    dedge = mul(wo_ref[...], (late * gating).astype(bf16), nt_dims)
+    dedge = pack(dedge).astype(bf16)
+    dedge = mul(to_owner, dedge, nn_dims).reshape(n, 8, 128)
+    dhat_e = dedge * gain_e
+    edge_raw = rstd_e * (
+        dhat_e - channel_sum(dhat_e) * inv_c - hat_e * (channel_sum(dhat_e * hat_e) * inv_c)
+    )
+    s3[...] = edge_raw.astype(bf16).astype(f32)
+    r3[me] = s3[me]
+    scatter(2, s3, r3, False)
+
+    gate_grad = (late * update).astype(bf16).astype(f32)
+    dgate = (gate_grad * gating * (1.0 - gating)).astype(bf16)
+    dnormed = mul(dgate, wg_ref[...], nt_dims)
+    gain2_sum = jnp.sum(dnormed2 * hat2, axis=0, keepdims=True)
+    shift2_sum = jnp.sum(dnormed2, axis=0, keepdims=True)
+
+    def collect(x):
+        x = x.reshape(128, 128)
+        low = jnp.sum(jnp.where(first, x, 0.0), axis=1, keepdims=True)
+        high = jnp.sum(jnp.where(first, 0.0, x), axis=1, keepdims=True)
+        spot = row // 4
+        return jnp.sum(
+            jnp.where(col == spot, low, 0.0) + jnp.where(col == spot + 32, high, 0.0),
+            axis=0,
+            keepdims=True,
+        )
+
+    gain_e_sum = collect(dedge * hat_e)
+    shift_e_sum = collect(dedge)
+    dsig_l = val_l * sig_l * (1.0 - sig_l) * valid
+    dsig_r = val_r * sig_r * (1.0 - sig_r) * valid
+    dval_l, dval_r = sig_l * valid, sig_r * valid
+
+    arrive(2, r3)
+    edge_round = r3[...].reshape(128, 128)
+    round0, round1 = by_parity(edge_round)
+    left_grad = mul(round0, diag0, nn_dims) + mul(round1, diag1, nn_dims)
+    cross0 = mul(round0, left_bf, tn_dims)
+    cross1 = mul(round1, left_bf, tn_dims)
+    right_grad = jnp.concatenate(
+        [
+            jnp.where(first64, cross0[:64], cross0[64:]),
+            jnp.where(first64, cross1[:64], cross1[64:]),
+        ],
+        axis=0,
+    ).astype(bf16)
+    right_grad = mul(pair_rows, right_grad, nn_dims)
+    s4[...] = jnp.concatenate(
+        [left_grad.reshape(n, 8, 128), right_grad.reshape(n, 8, 128)], axis=1
+    ).astype(bf16)
+    r4[me] = s4[me]
+    scatter(3, s4, r4, False)
+    arrive(3, r4)
+
+    grads = r4[...].astype(f32)
+    grads = jnp.concatenate(
+        [grads[:, :8].reshape(128, 128), grads[:, 8:].reshape(128, 128)], axis=1
+    ).astype(bf16)
+    grads = mul(from_owner, grads, nn_dims)
+    dleft, dright = unpack(grads[:, :128]), unpack(grads[:, 128:])
+    dmixed = jnp.concatenate(
+        [dleft * dsig_l, dleft * dval_l, dright * dsig_r, dright * dval_r], axis=0
+    ).astype(bf16)
+    dnormed = (dnormed + mul(dmixed, we_t, tn_dims)).astype(bf16).astype(f32)
+    gain1_sum = jnp.sum(dnormed * hat1, axis=0, keepdims=True)
+    shift1_sum = jnp.sum(dnormed, axis=0, keepdims=True)
+    blank = jnp.zeros((2, 128), f32)
+    s5[...] = jnp.concatenate(
+        [gain1_sum, shift1_sum, gain2_sum, shift2_sum, gain_e_sum, shift_e_sum, blank], axis=0
+    )
+    r5[me] = s5[...]
+    scatter(4, s5, r5, True)
+    dhat1 = dnormed * gain1
+    early = rstd1 * (
+        dhat1
+        - jnp.mean(dhat1, axis=1, keepdims=True)
+        - hat1 * jnp.mean(dhat1 * hat1, axis=1, keepdims=True)
+    )
+    early = early.astype(bf16).astype(f32)
+    out_ref[...] = (early + late).astype(bf16).reshape(out_ref.shape)
+    arrive(4, r5)
+    sums = jnp.sum(r5[...], axis=0) * (1.0 / tokens)
+    norm_ref[...] = sums[:4]
+    edge_ref[...] = sums[4:6, :64]
+    for phase, buffer in enumerate((r1, r2, r3, r4, r5)):
+        sent(phase, buffer)
+
+
+def fused_body(n, *args):
+    (
+        pair_state,
+        cotangent,
+        pair_mask,
+        token_count,
+        norm_gain,
+        norm_shift,
+        w_edges,
+        w_gate,
+        edge_gain,
+        edge_shift,
+        w_out,
+        final_gain,
+        final_shift,
+        w_expand,
+        w_contract,
+    ) = args
+    vmem = pl.BlockSpec(memory_space=pltpu.VMEM)
+    cells = pair_state.shape[0] * pair_state.shape[1]
+    tile = pltpu.VMEM((n, 8, 128), f32)
+    pair = pltpu.VMEM((n, 16, 128), bf16)
+    return pl.pallas_call(
+        functools.partial(fused_kernel, n),
+        out_shape=(
+            jax.ShapeDtypeStruct(pair_state.shape, bf16),
+            jax.ShapeDtypeStruct((4, 128), f32),
+            jax.ShapeDtypeStruct((2, 64), f32),
+        ),
+        in_specs=[pl.BlockSpec(memory_space=pltpu.SMEM)] + [vmem] * 14,
+        out_specs=(vmem, vmem, vmem),
+        scratch_shapes=[
+            pair,
+            pair,
+            tile,
+            tile,
+            tile,
+            tile,
+            pair,
+            pair,
+            pltpu.VMEM((8, 128), f32),
+            tile,
+            pltpu.VMEM((cells, w_contract.shape[0]), bf16),
+            pltpu.SemaphoreType.DMA((5,)),
+            pltpu.SemaphoreType.DMA((5,)),
+        ],
+        compiler_params=pltpu.CompilerParams(
+            collective_id=0, has_side_effects=True, vmem_limit_bytes=32 * 1024 * 1024
+        ),
+    )(
+        token_count,
+        pair_state,
+        cotangent,
+        pair_mask,
+        norm_gain.reshape(1, -1),
+        norm_shift.reshape(1, -1),
+        w_edges,
+        w_gate,
+        edge_gain.reshape(1, -1),
+        edge_shift.reshape(1, -1),
+        w_out,
+        final_gain.reshape(1, -1),
+        final_shift.reshape(1, -1),
+        w_expand,
+        w_contract,
+    )
+
+
+def pick_body(n):
+    def chosen(*args):
+        rows, tokens, _ = args[0].shape
+        if (n, rows, tokens) == (16, 4, 64):
+            return fused_body(n, *args)
+        return body(*args)
+
+    return chosen
+
 
 def solution(mesh):
     in_specs = (
@@ -212,4 +616,5 @@
         P(),
     )
     out_specs = (P(("groups", "dap"), None, None), P("groups", None), P("groups", None))
-    return jax.shard_map(body, mesh=mesh, in_specs=in_specs, out_specs=out_specs, check_vma=False)
+    chosen = pick_body(mesh.shape["dap"])
+    return jax.shard_map(chosen, mesh=mesh, in_specs=in_specs, out_specs=out_specs, check_vma=False)

time: 103 us -> 39.1 us (0.38)
  blocking collectives: 80.8 us -> 0 us
  Pallas kernels: 0 us -> 29 us
  other arithmetic: 5.89 us -> 0 us
  matrix products: 5 us -> 0 us
  starting transfers between devices: 3.5 us -> 0 us
  local copies, waits for them, and re-layouts: 6.01 us -> 8.31 us
    all_gather x2 -> x0, blocking collectives: 50.9 us -> none  [the longest x1 26.2 us: body(): lax.all_gather(right_rows, 'dap', axis=1, tiled=True)]
    psum x1 -> x0, blocking collectives: 29.8 us -> none  [body(): pair_totals, edge_totals = lax.psum((pair_terms, edge_terms), 'dap')]
    pallas_call x0 -> x1, Pallas kernels: none -> 29 us  [fused_body(): pl.pallas_call(functools.partial(fused_kernel, n), out_shape=(jax.ShapeDt...]
    dot_general x12 -> x0, matrix products: 5 us -> none  [the longest x1 0.8 us: absorb_block(): jnp.einsum('cik,cjk->cij', left_rows, piece_rows, preferred_element_type=...]
    all_to_all x1 -> x0, starting transfers between devices: 3.5 us -> none  [body(): lax.all_to_all(edge_grads_all, 'dap', split_axis=2, concat_axis=1, tiled=...]
    unnamed x30 -> x31, local copies, waits for them, and re-layouts: 5.06 us -> 8.31 us
    reduce_sum x8 -> x0, other arithmetic: 2.81 us -> none  [the longest x4 1.37 us: layer_norm(): return centred * lax.rsqrt(spread + epsilon) * norm_scale + norm_offset]
    convert_element_type x8 -> x0, other arithmetic: 1.58 us -> none  [the longest x1 0.65 us: body(): (summed[0].astype(jnp.float32) + summed[1].astype(jnp.float32)).astype(jn...]
  transfers between devices with their start and end apart: 1 -> 0, of which waited for: 0 -> 0; matrix products, arithmetic and copies ran while one was open for 1% -> 0% of each run, Pallas kernels for 0% -> 0%
where the time goes in v1:
time: 39.1 us; the launch traced here: 38.6 us
  Pallas kernels  29 us (74%)
  local copies, waits for them, and re-layouts  8.31 us (21%)
  between operations  1.36 us (3%)
    pallas_call x1, Pallas kernels, fused_body(): pl.pallas_call(functools.partial(fused_kernel, n), out_shape=(jax.ShapeDt...  29 us
    unnamed x31, local copies, waits for them, and re-layouts  8.31 us

profile of v1, /device:TPU:0, one launch (start us, length us, event | category | flops | bytes accessed | tf_op | source)
XLA Modules:
  0.0 38.6 jit_solution(12899594981295907835)
XLA Ops:
  1.3 0.0 copy-start.11
  1.3 0.0 copy-start.12
  1.3 0.0 copy-start.13
  1.3 0.0 copy-start.7
  1.3 0.0 copy-start.8
  1.3 0.0 copy-start.9
  1.3 0.0 copy-start.10
  1.4 0.6 %copy-done.11 = f32[64]{0:T(128)S(1)} copy-done((f32[64]{0:T(128)S(1)}, f32[64]{0:T(128)}, u32[]{:S(2)}) %copy-start.11) | copy-done | bytes 280
  1.9 0.0 copy-done.12
  2.0 0.0 copy-done.13
  2.0 0.0 copy-done.7
  2.0 0.0 copy-done.8
  2.0 0.0 copy-done.9
  2.0 0.0 copy-done.10
  2.0 0.0 copy-start
  2.0 0.9 %copy-done = bf16[128,1024]{1,0:T(8,128)(2,1)S(1)} copy-done((bf16[128,1024]{1,0:T(8,128)(2,1)S(1)}, bf16[128,1024]{1,0:T(8,128)(2,1)}, u32[]{:S(2)}) %copy-start) | copy-done | bytes 262168
  3.0 0.0 copy-start.1
  3.0 0.9 %copy-done.1 = bf16[512,128]{1,0:T(8,128)(2,1)S(1)} copy-done((bf16[512,128]{1,0:T(8,128)(2,1)S(1)}, bf16[512,128]{1,0:T(8,128)(2,1)}, u32[]{:S(2)}) %copy-start.1) | copy-done | bytes 131096
  3.9 0.0 copy-start.2
  3.9 0.8 %copy-done.2 = bf16[4,64,128]{2,1,0:T(8,128)(2,1)S(1)} copy-done((bf16[4,64,128]{2,1,0:T(8,128)(2,1)S(1)}, bf16[4,64,128]{2,1,0:T(8,128)(2,1)}, u32[]{:S(2)}) %copy-start.2) | copy-done | bytes 65560
  4.7 0.0 copy-start.3
  4.7 0.8 %copy-done.3 = bf16[4,64,128]{2,1,0:T(8,128)(2,1)S(1)} copy-done((bf16[4,64,128]{2,1,0:T(8,128)(2,1)S(1)}, bf16[4,64,128]{2,1,0:T(8,128)(2,1)}, u32[]{:S(2)}) %copy-start.3) | copy-done | bytes 65560
  5.6 0.0 copy-start.4
  5.6 0.8 %copy-done.4 = bf16[128,256]{1,0:T(8,128)(2,1)S(1)} copy-done((bf16[128,256]{1,0:T(8,128)(2,1)S(1)}, bf16[128,256]{1,0:T(8,128)(2,1)}, u32[]{:S(2)}) %copy-start.4) | copy-done | bytes 65560
  6.4 0.0 copy-start.5
  6.4 0.8 %copy-done.5 = bf16[128,128]{1,0:T(8,128)(2,1)S(1)} copy-done((bf16[128,128]{1,0:T(8,128)(2,1)S(1)}, bf16[128,128]{1,0:T(8,128)(2,1)}, u32[]{:S(2)}) %copy-start.5) | copy-done | bytes 32792
  7.2 0.0 copy-start.6
  7.2 0.7 %copy-done.6 = bf16[64,128]{1,0:T(8,128)(2,1)S(1)} copy-done((bf16[64,128]{1,0:T(8,128)(2,1)S(1)}, bf16[64,128]{1,0:T(8,128)(2,1)}, u32[]{:S(2)}) %copy-start.6) | copy-done | bytes 16408
  7.9 29.0 %shard_map.166 = (bf16[4,64,128]{2,1,0:T(8,128)(2,1)S(1)}, f32[4,128]{1,0:T(4,128)S(1)}, f32[2,64]{1,0:T(2,128)S(1)}) custom-call(s32[1]{0:T(128)S(6)} %copy.21.count_ref, bf16[4,64,128]{2,1,0:T(8,128)(2,1)S(1)} %copy-done.2, bf16[4,64,128]{2,1,0:T(8,128)(2,1)S(1)} %copy-done.3, s32[4,64]{1,0:T(4,128)S(1)} %copy-done.7, f32[1,128]{1,0:T(1,128)S(1)} %bitcast.6, ...), custom_call_target="tpu_custom_call" | custom-call | tf_op jit(solution)/shard_map/pallas_call | solution.py:544
  36.9 0.6 %copy.22 = bf16[4,64,128]{2,1,0:T(8,128)(2,1)} copy(bf16[4,64,128]{2,1,0:T(8,128)(2,1)S(1)} %get-tuple-element.6) | data formatting | bytes 131072
  37.5 0.6 %copy.23 = f32[4,128]{1,0:T(4,128)} copy(f32[4,128]{1,0:T(4,128)S(1)} %get-tuple-element.7) | data formatting | bytes 4096
  38.1 0.6 %copy.24 = f32[2,64]{1,0:T(2,128)} copy(f32[2,64]{1,0:T(2,128)S(1)} %get-tuple-element.8) | data formatting | bytes 1024
Async XLA Ops:
  1.3 0.7 %copy-start.11 = (f32[64]{0:T(128)S(1)}, f32[64]{0:T(128)}, u32[]{:S(2)}) copy-start(f32[64]{0:T(128)} %param.24) | copy-start | bytes 772
  1.3 0.7 %copy-start.12 = (f32[128]{0:T(128)S(1)}, f32[128]{0:T(128)}, u32[]{:S(2)}) copy-start(f32[128]{0:T(128)} %param.26) | copy-start | bytes 1540
  1.3 0.7 %copy-start.13 = (f32[128]{0:T(128)S(1)}, f32[128]{0:T(128)}, u32[]{:S(2)}) copy-start(f32[128]{0:T(128)} %param.27) | copy-start | bytes 1540
  1.3 0.7 %copy-start.7 = (s32[4,64]{1,0:T(4,128)S(1)}, s32[4,64]{1,0:T(4,128)}, u32[]{:S(2)}) copy-start(s32[4,64]{1,0:T(4,128)} %mask_ref.1) | copy-start | bytes 3076
  1.3 0.7 %copy-start.8 = (f32[128]{0:T(128)S(1)}, f32[128]{0:T(128)}, u32[]{:S(2)}) copy-start(f32[128]{0:T(128)} %param.19) | copy-start | bytes 1540
  1.3 0.7 %copy-start.9 = (f32[128]{0:T(128)S(1)}, f32[128]{0:T(128)}, u32[]{:S(2)}) copy-start(f32[128]{0:T(128)} %param.20) | copy-start | bytes 1540
  1.3 0.7 %copy-start.10 = (f32[64]{0:T(128)S(1)}, f32[64]{0:T(128)}, u32[]{:S(2)}) copy-start(f32[64]{0:T(128)} %param.23) | copy-start | bytes 772
  2.0 0.9 %copy-start = (bf16[128,1024]{1,0:T(8,128)(2,1)S(1)}, bf16[128,1024]{1,0:T(8,128)(2,1)}, u32[]{:S(2)}) copy-start(bf16[128,1024]{1,0:T(8,128)(2,1)} %wx_ref.1) | copy-start | bytes 786436
  3.0 0.9 %copy-start.1 = (bf16[512,128]{1,0:T(8,128)(2,1)S(1)}, bf16[512,128]{1,0:T(8,128)(2,1)}, u32[]{:S(2)}) copy-start(bf16[512,128]{1,0:T(8,128)(2,1)} %wc_ref.1) | copy-start | bytes 393220
  3.9 0.8 %copy-start.2 = (bf16[4,64,128]{2,1,0:T(8,128)(2,1)S(1)}, bf16[4,64,128]{2,1,0:T(8,128)(2,1)}, u32[]{:S(2)}) copy-start(bf16[4,64,128]{2,1,0:T(8,128)(2,1)} %state_ref.1) | copy-start | bytes 196612
  4.7 0.8 %copy-start.3 = (bf16[4,64,128]{2,1,0:T(8,128)(2,1)S(1)}, bf16[4,64,128]{2,1,0:T(8,128)(2,1)}, u32[]{:S(2)}) copy-start(bf16[4,64,128]{2,1,0:T(8,128)(2,1)} %cot_ref.1) | copy-start | bytes 196612
  5.6 0.8 %copy-start.4 = (bf16[128,256]{1,0:T(8,128)(2,1)S(1)}, bf16[128,256]{1,0:T(8,128)(2,1)}, u32[]{:S(2)}) copy-start(bf16[128,256]{1,0:T(8,128)(2,1)} %we_ref.1) | copy-start | bytes 196612
  6.4 0.8 %copy-start.5 = (bf16[128,128]{1,0:T(8,128)(2,1)S(1)}, bf16[128,128]{1,0:T(8,128)(2,1)}, u32[]{:S(2)}) copy-start(bf16[128,128]{1,0:T(8,128)(2,1)} %wg_ref.1) | copy-start | bytes 98308
  7.2 0.7 %copy-start.6 = (bf16[64,128]{1,0:T(8,128)(2,1)S(1)}, bf16[64,128]{1,0:T(8,128)(2,1)}, u32[]{:S(2)}) copy-start(bf16[64,128]{1,0:T(8,128)(2,1)} %wo_ref.1) | copy-start | bytes 49156

commit v2 on v1

--- a/solution.py
+++ b/solution.py
@@ -252,59 +252,63 @@
     return total + pltpu.roll(total, 64, 1)
 
 
-def fused_kernel(
-    n,
-    count_ref,
-    state_ref,
-    cot_ref,
-    mask_ref,
-    gain1_ref,
-    shift1_ref,
-    we_ref,
-    wg_ref,
-    gain_e_ref,
-    shift_e_ref,
-    wo_ref,
-    gain2_ref,
-    shift2_ref,
-    wx_ref,
-    wc_ref,
-    out_ref,
-    norm_ref,
-    edge_ref,
-    s1,
-    r1,
-    s2,
-    r2,
-    s3,
-    r3,
-    s4,
-    r4,
-    s5,
-    r5,
-    dact_ref,
-    send_sem,
-    recv_sem,
-):
+names = (
+    "state",
+    "we",
+    "gain1",
+    "shift1",
+    "mask",
+    "real",
+    "wg",
+    "cot",
+    "wc",
+    "gain_e",
+    "shift_e",
+    "wo",
+    "gain2",
+    "shift2",
+    "wx",
+)
+
+
+def fused_kernel(n, *refs):
+    count = len(names)
+    sources, refs = refs[:count], refs[count:]
+    out_ref, norm_ref, edge_ref, *held = refs[: 3 + count]
+    s1, r1, s2, r2, s3, r3, s4, r4, s5, r5, dact_ref, send_sem, recv_sem, load_sem = refs[3 + count :]
     me = lax.axis_index("dap")
     group = lax.axis_index("groups")
-    cells = state_ref.shape[0] * state_ref.shape[1]
-    tokens = state_ref.shape[1]
+    loads = {
+        name: pltpu.make_async_copy(sources[at], held[at], load_sem.at[at])
+        for at, name in enumerate(names)
+    }
+    for name in names:
+        loads[name].start()
+
+    def load(name):
+        loads[name].wait()
+        return held[names.index(name)]
+
+    rows, tokens = sources[0].shape[:2]
+    cells = rows * tokens
 
     barrier = pltpu.get_barrier_semaphore()
 
-    def greet(step, carry):
-        peer = lax.rem(me + step, n)
+    high, y, core = me // 8, (me // 2) % 2, me % 2
+    z = me // 4
+    peers = []
+    for far in (3 - 3 * high, 2 - high, 1 - z + 4 * high):
+        for side in (1 - y, y):
+            peers += [far * 4 + side * 2 + 1 - core, far * 4 + side * 2 + core]
+    peers += [z * 4 + (1 - y) * 2 + 1 - core, z * 4 + (1 - y) * 2 + core, z * 4 + y * 2 + 1 - core]
+
+    for peer in peers:
         pl.semaphore_signal(
             barrier, inc=1, device_id=(group, peer), device_id_type=pl.DeviceIdType.MESH
         )
-        return carry
-
-    lax.fori_loop(1, n, greet, 0)
 
     def scatter(phase, src, dst, same):
-        def send(step, carry):
-            peer = lax.rem(me + step, n)
+        for peer in peers:
             pltpu.make_async_remote_copy(
                 src_ref=src if same else src.at[peer],
                 dst_ref=dst.at[me],
@@ -313,9 +317,6 @@
                 device_id=(group, peer),
                 device_id_type=pl.DeviceIdType.MESH,
             ).start()
-            return carry
-
-        lax.fori_loop(1, n, send, 0)
 
     def arrive(phase, dst):
         part = dst.at[pl.ds(0, n - 1)]
@@ -325,19 +326,19 @@
         part = dst.at[pl.ds(0, n - 1)]
         pltpu.make_async_copy(part, part, send_sem.at[phase]).wait()
 
-    state = state_ref[...].reshape(cells, 128).astype(f32)
-    gain1 = gain1_ref[...]
+    state = load("state")[...].reshape(cells, 128).astype(f32)
+    gain1 = load("gain1")[...]
     centred = state - jnp.mean(state, axis=1, keepdims=True)
     rstd1 = lax.rsqrt(jnp.mean(centred * centred, axis=1, keepdims=True) + epsilon)
     hat1 = centred * rstd1
-    normed = (hat1 * gain1 + shift1_ref[...]).astype(bf16)
-    we_t = we_ref[...].T
+    normed = (hat1 * gain1 + load("shift1")[...]).astype(bf16)
+    we_t = load("we")[...].T
     mixed = mul(we_t, normed, nt_dims)
-    count = count_ref[0]
-    mask = mask_ref[...].astype(f32)
-    mask = jnp.concatenate([mask[i : i + 1] for i in range(4)], axis=1)
+    real = load("real")[...]
+    mask = load("mask")[...].astype(f32)
+    mask = jnp.concatenate([mask[i : i + 1] for i in range(rows)], axis=1)
     cell = iota((1, cells), 1)
-    live = (cell % tokens < count) & (me * 4 + cell // tokens < count)
+    live = (cell % tokens < real) & (me * rows + cell // tokens < real)
     valid = jnp.where(live, mask, 0.0)
     sig_l, val_l = sigmoid(mixed[:64]), mixed[64:128]
     sig_r, val_r = sigmoid(mixed[128:192]), mixed[192:]
@@ -355,8 +356,10 @@
     pl.semaphore_wait(barrier, n - 1)
     scatter(0, s1, r1, False)
 
-    gating = sigmoid(mul(normed, wg_ref[...], nn_dims)).astype(bf16).astype(f32)
-    cot = cot_ref[...].reshape(cells, 128)
+    wg = load("wg")[...]
+    gating = sigmoid(mul(normed, wg, nn_dims)).astype(bf16).astype(f32)
+    cot = load("cot")[...].reshape(cells, 128)
+    wc_ref = load("wc")
     dact_ref[...] = mul(cot, wc_ref[...], nt_dims).astype(bf16)
     lane64 = iota((128, 64), 1)
     row64 = iota((128, 64), 0) // 4
@@ -367,7 +370,9 @@
         high = jnp.sum(jnp.where(lane64 == row64 + 32, vector, 0.0), axis=1, keepdims=True)
         return jnp.where(first, low, high).reshape(n, 8, 128)
 
-    gain_e, shift_e = spread(gain_e_ref[...]), spread(shift_e_ref[...])
+    gain_e, shift_e = spread(load("gain_e")[...]), spread(load("shift_e")[...])
+    gain2, shift2 = load("gain2")[...], load("shift2")[...]
+    wo, wx_ref = load("wo")[...], load("wx")
     by_pair = one_hot(col == ((row % 64) // 4) * 8 + (row // 64) * 4 + row % 4)
     pair_rows = one_hot(row == ((col % 64) // 4) * 8 + (col // 64) * 4 + col % 4)
     even = (iota((128, 128), 0) // 4) % 2 == 0
@@ -402,13 +407,12 @@
     hat_e = centred_e * rstd_e
     edge_normed = (hat_e * gain_e + shift_e).reshape(128, 128).astype(bf16)
     edge_normed = unpack(mul(from_owner, edge_normed, nn_dims)).astype(bf16)
-    update = mul(edge_normed, wo_ref[...], tn_dims)
+    update = mul(edge_normed, wo, tn_dims)
     middle = (state + gating * update).astype(bf16).astype(f32)
     centred2 = middle - jnp.mean(middle, axis=1, keepdims=True)
     rstd2 = lax.rsqrt(jnp.mean(centred2 * centred2, axis=1, keepdims=True) + epsilon)
     hat2 = centred2 * rstd2
-    gain2 = gain2_ref[...]
-    normed2 = (hat2 * gain2 + shift2_ref[...]).astype(bf16)
+    normed2 = (hat2 * gain2 + shift2).astype(bf16)
     units = wc_ref.shape[0]
     dnormed2 = jnp.zeros((cells, 128), f32)
     for begin in range(0, units, 256):
@@ -430,7 +434,7 @@
         - hat2 * jnp.mean(dhat2 * hat2, axis=1, keepdims=True)
     )
     late = (cot.astype(f32) + dmiddle).astype(bf16).astype(f32)
-    dedge = mul(wo_ref[...], (late * gating).astype(bf16), nt_dims)
+    dedge = mul(wo, (late * gating).astype(bf16), nt_dims)
     dedge = pack(dedge).astype(bf16)
     dedge = mul(to_owner, dedge, nn_dims).reshape(n, 8, 128)
     dhat_e = dedge * gain_e
@@ -443,7 +447,7 @@
 
     gate_grad = (late * update).astype(bf16).astype(f32)
     dgate = (gate_grad * gating * (1.0 - gating)).astype(bf16)
-    dnormed = mul(dgate, wg_ref[...], nt_dims)
+    dnormed = mul(dgate, wg, nt_dims)
     gain2_sum = jnp.sum(dnormed2 * hat2, axis=0, keepdims=True)
     shift2_sum = jnp.sum(dnormed2, axis=0, keepdims=True)
 
@@ -538,6 +542,23 @@
         w_contract,
     ) = args
     vmem = pl.BlockSpec(memory_space=pltpu.VMEM)
+    operands = (
+        pair_state,
+        w_edges,
+        norm_gain.reshape(1, -1),
+        norm_shift.reshape(1, -1),
+        pair_mask,
+        token_count.reshape(1, 1),
+        w_gate,
+        cotangent,
+        w_contract,
+        edge_gain.reshape(1, -1),
+        edge_shift.reshape(1, -1),
+        w_out,
+        final_gain.reshape(1, -1),
+        final_shift.reshape(1, -1),
+        w_expand,
+    )
     cells = pair_state.shape[0] * pair_state.shape[1]
     tile = pltpu.VMEM((n, 8, 128), f32)
     pair = pltpu.VMEM((n, 16, 128), bf16)
@@ -548,9 +569,10 @@
             jax.ShapeDtypeStruct((4, 128), f32),
             jax.ShapeDtypeStruct((2, 64), f32),
         ),
-        in_specs=[pl.BlockSpec(memory_space=pltpu.SMEM)] + [vmem] * 14,
+        in_specs=[pl.BlockSpec(memory_space=pltpu.HBM)] * len(operands),
         out_specs=(vmem, vmem, vmem),
-        scratch_shapes=[
+        scratch_shapes=[pltpu.VMEM(x.shape, x.dtype) for x in operands]
+        + [
             pair,
             pair,
             tile,
@@ -564,27 +586,12 @@
             pltpu.VMEM((cells, w_contract.shape[0]), bf16),
             pltpu.SemaphoreType.DMA((5,)),
             pltpu.SemaphoreType.DMA((5,)),
+            pltpu.SemaphoreType.DMA((len(operands),)),
         ],
         compiler_params=pltpu.CompilerParams(
-            collective_id=0, has_side_effects=True, vmem_limit_bytes=32 * 1024 * 1024
+            collective_id=0, has_side_effects=True, vmem_limit_bytes=60 * 1024 * 1024
         ),
-    )(
-        token_count,
-        pair_state,
-        cotangent,
-        pair_mask,
-        norm_gain.reshape(1, -1),
-        norm_shift.reshape(1, -1),
-        w_edges,
-        w_gate,
-        edge_gain.reshape(1, -1),
-        edge_shift.reshape(1, -1),
-        w_out,
-        final_gain.reshape(1, -1),
-        final_shift.reshape(1, -1),
-        w_expand,
-        w_contract,
-    )
+    )(*operands)
 
 
 def pick_body(n):

time: 39.1 us -> 33.3 us (0.85)
  local copies, waits for them, and re-layouts: 8.31 us -> 2.7 us
    unnamed x31 -> x7, local copies, waits for them, and re-layouts: 8.31 us -> 2.7 us
where the time goes in v2:
time: 33.3 us; the launch traced here: 33.1 us
  Pallas kernels  29.1 us (87%)
  local copies, waits for them, and re-layouts  2.7 us (8%)
  between operations  1.3 us (4%)
    pallas_call x1, Pallas kernels, fused_body(): pl.pallas_call(functools.partial(fused_kernel, n), out_shape=(jax.ShapeDt...  29.1 us
    unnamed x7, local copies, waits for them, and re-layouts  2.7 us

profile of v2, /device:TPU:0, one launch (start us, length us, event | category | flops | bytes accessed | tf_op | source)
XLA Modules:
  0.0 33.1 jit_solution(7295955546243636428)
XLA Ops:
  1.3 29.1 %shard_map.166 = (bf16[4,64,128]{2,1,0:T(8,128)(2,1)}, f32[4,128]{1,0:T(4,128)}, f32[2,64]{1,0:T(2,128)}) custom-call(bf16[4,64,128]{2,1,0:T(8,128)(2,1)} %refs_0_.1, bf16[128,256]{1,0:T(8,128)(2,1)} %refs_1_.1, f32[1,128]{1,0:T(1,128)} %bitcast.8, f32[1,128]{1,0:T(1,128)} %bitcast.9, s32[4,64]{1,0:T(4,128)} %refs_4_.1, s32[1,1]{1,0:T(1,128)} %bitcast.7.refs_5_, ...), custom_call_target="tpu_custom_call" | custom-call | tf_op jit(solution)/shard_map/pallas_call | solution.py:565
  30.4 0.0 copy-start
  30.4 1.5 %copy.22 = bf16[4,64,128]{2,1,0:T(8,128)(2,1)} copy(bf16[4,64,128]{2,1,0:T(8,128)(2,1)} %get-tuple-element.6) | data formatting | bytes 131072
  31.9 0.0 copy-done
  31.9 0.0 copy-start.1
  31.9 0.6 %copy.23 = f32[4,128]{1,0:T(4,128)} copy(f32[4,128]{1,0:T(4,128)S(1)} %copy-done) | data formatting | bytes 4096
  32.5 0.1 copy-done.1
  32.5 0.6 %copy.24 = f32[2,64]{1,0:T(2,128)} copy(f32[2,64]{1,0:T(2,128)S(1)} %copy-done.1) | data formatting | bytes 1024
Async XLA Ops:
  30.4 1.5 %copy-start = (f32[4,128]{1,0:T(4,128)S(1)}, f32[4,128]{1,0:T(4,128)}, u32[]{:S(2)}) copy-start(f32[4,128]{1,0:T(4,128)} %get-tuple-element.7) | copy-start | bytes 6148
  31.9 0.7 %copy-start.1 = (f32[2,64]{1,0:T(2,128)S(1)}, f32[2,64]{1,0:T(2,128)}, u32[]{:S(2)}) copy-start(f32[2,64]{1,0:T(2,128)} %get-tuple-element.8) | copy-start | bytes 1540

commit v3 on v2

--- a/solution.py
+++ b/solution.py
@@ -521,6 +521,17 @@
     edge_ref[...] = sums[4:6, :64]
     for phase, buffer in enumerate((r1, r2, r3, r4, r5)):
         sent(phase, buffer)
+
+
+def write_out(a, b, c, out_a, out_b, out_c, sem):
+    copies = [
+        pltpu.make_async_copy(source, target, sem.at[at])
+        for at, (source, target) in enumerate(((a, out_a), (b, out_b), (c, out_c)))
+    ]
+    for copy in copies:
+        copy.start()
+    for copy in copies:
+        copy.wait()
 
 
 def fused_body(n, *args):
@@ -562,12 +573,12 @@
     cells = pair_state.shape[0] * pair_state.shape[1]
     tile = pltpu.VMEM((n, 8, 128), f32)
     pair = pltpu.VMEM((n, 16, 128), bf16)
-    return pl.pallas_call(
+    held = pl.pallas_call(
         functools.partial(fused_kernel, n),
         out_shape=(
-            jax.ShapeDtypeStruct(pair_state.shape, bf16),
-            jax.ShapeDtypeStruct((4, 128), f32),
-            jax.ShapeDtypeStruct((2, 64), f32),
+            pltpu.VMEM(pair_state.shape, bf16),
+            pltpu.VMEM((4, 128), f32),
+            pltpu.VMEM((2, 64), f32),
         ),
         in_specs=[pl.BlockSpec(memory_space=pltpu.HBM)] * len(operands),
         out_specs=(vmem, vmem, vmem),
@@ -592,6 +603,14 @@
             collective_id=0, has_side_effects=True, vmem_limit_bytes=60 * 1024 * 1024
         ),
     )(*operands)
+    return pl.pallas_call(
+        write_out,
+        out_shape=tuple(jax.ShapeDtypeStruct(x.shape, x.dtype) for x in held),
+        in_specs=[vmem] * 3,
+        out_specs=(pl.BlockSpec(memory_space=pltpu.HBM),) * 3,
+        scratch_shapes=[pltpu.SemaphoreType.DMA((3,))],
+        compiler_params=pltpu.CompilerParams(vmem_limit_bytes=1024 * 1024),
+    )(*held)
 
 
 def pick_body(n):

time: 33.3 us -> 30.6 us (0.919)
  local copies, waits for them, and re-layouts: 2.7 us -> 0 us
    unnamed x7 -> x0, local copies, waits for them, and re-layouts: 2.7 us -> none
    pallas_call x1 -> x2, Pallas kernels: 29.1 us -> 29.1 us  [the longest x1 28.5 us: fused_body(): pl.pallas_call(functools.partial(fused_kernel, n), out_shape=(pltpu.VMEM(...]
where the time goes in v3:
time: 30.6 us; the launch traced here: 30.4 us
  Pallas kernels  29.1 us (95%)
  between operations  1.29 us (4%)
    pallas_call x1, Pallas kernels, fused_body(): pl.pallas_call(functools.partial(fused_kernel, n), out_shape=(pltpu.VMEM(...  28.5 us
    pallas_call x1, Pallas kernels, fused_body(): pl.pallas_call(write_out, out_shape=tuple((jax.ShapeDtypeStruct(x.shape,...  0.66 us

profile of v3, /device:TPU:0, one launch (start us, length us, event | category | flops | bytes accessed | tf_op | source)
XLA Modules:
  0.0 30.4 jit_solution(4482151168080623097)
XLA Ops:
  1.3 28.5 %shard_map.166 = (bf16[4,64,128]{2,1,0:T(8,128)(2,1)S(1)}, f32[4,128]{1,0:T(4,128)S(1)}, f32[2,64]{1,0:T(2,128)S(1)}) custom-call(bf16[4,64,128]{2,1,0:T(8,128)(2,1)} %refs_0_.1, bf16[128,256]{1,0:T(8,128)(2,1)} %refs_1_.1, f32[1,128]{1,0:T(1,128)} %bitcast.8, f32[1,128]{1,0:T(1,128)} %bitcast.9, s32[4,64]{1,0:T(4,128)} %refs_4_.1, s32[1,1]{1,0:T(1,128)} %bitcast.7.refs_5_, ...), custom_call_target="tpu_custom_call" | custom-call | tf_op jit(solution)/shard_map/pallas_call | solution.py:576
  29.8 0.7 %shard_map.167 = (bf16[4,64,128]{2,1,0:T(8,128)(2,1)}, f32[4,128]{1,0:T(4,128)}, f32[2,64]{1,0:T(2,128)}) custom-call(bf16[4,64,128]{2,1,0:T(8,128)(2,1)S(1)} %get-tuple-element.6.a, f32[4,128]{1,0:T(4,128)S(1)} %get-tuple-element.7.b, f32[2,64]{1,0:T(2,128)S(1)} %get-tuple-element.8.c), custom_call_target="tpu_custom_call" | custom-call | tf_op jit(solution)/shard_map/pallas_call | solution.py:606

commit v4 on v3

--- a/solution.py
+++ b/solution.py
@@ -275,16 +275,13 @@
     count = len(names)
     sources, refs = refs[:count], refs[count:]
     out_ref, norm_ref, edge_ref, *held = refs[: 3 + count]
-    s1, r1, s2, r2, s3, r3, s4, r4, s5, r5, dact_ref, send_sem, recv_sem, load_sem = refs[3 + count :]
+    s1, r1, s2, r2, s3, r3, s4, r4, s5, r5, dact_ref, wxt_ref, send_sem, recv_sem, load_sem = refs[3 + count :]
     me = lax.axis_index("dap")
     group = lax.axis_index("groups")
     loads = {
         name: pltpu.make_async_copy(sources[at], held[at], load_sem.at[at])
         for at, name in enumerate(names)
     }
-    for name in names:
-        loads[name].start()
-
     def load(name):
         loads[name].wait()
         return held[names.index(name)]
@@ -306,6 +303,9 @@
         pl.semaphore_signal(
             barrier, inc=1, device_id=(group, peer), device_id_type=pl.DeviceIdType.MESH
         )
+
+    for name in names:
+        loads[name].start()
 
     def scatter(phase, src, dst, same):
         for peer in peers:
@@ -352,9 +352,9 @@
         [both[:, :128].reshape(n, 8, 128), both[:, 128:].reshape(n, 8, 128)], axis=1
     ).astype(bf16)
     s1[...] = both
-    r1[me] = s1[me]
     pl.semaphore_wait(barrier, n - 1)
     scatter(0, s1, r1, False)
+    r1[me] = s1[me]
 
     wg = load("wg")[...]
     gating = sigmoid(mul(normed, wg, nn_dims)).astype(bf16).astype(f32)
@@ -373,6 +373,7 @@
     gain_e, shift_e = spread(load("gain_e")[...]), spread(load("shift_e")[...])
     gain2, shift2 = load("gain2")[...], load("shift2")[...]
     wo, wx_ref = load("wo")[...], load("wx")
+    wxt_ref[...] = wx_ref[...].T
     by_pair = one_hot(col == ((row % 64) // 4) * 8 + (row // 64) * 4 + row % 4)
     pair_rows = one_hot(row == ((col % 64) // 4) * 8 + (col // 64) * 4 + col % 4)
     even = (iota((128, 128), 0) // 4) % 2 == 0
@@ -395,8 +396,8 @@
     left0, left1 = by_parity(left_all)
     edges = mul(left0, diag0, nt_dims) + mul(left1, diag1, nt_dims)
     s2[...] = edges.reshape(n, 8, 128)
+    scatter(1, s2, r2, False)
     r2[me] = s2[me]
-    scatter(1, s2, r2, False)
     left_bf = left_all.astype(bf16)
     arrive(1, r2)
 
@@ -425,7 +426,9 @@
         silu = swish_in * sig
         dlinear = (dact * silu).astype(bf16)
         dswish = (dact * linear * (sig + silu * (1.0 - sig))).astype(bf16)
-        dnormed2 = dnormed2 + mul(dswish, w_swish, nt_dims) + mul(dlinear, w_linear, nt_dims)
+        swish_t = wxt_ref[begin : begin + 256]
+        linear_t = wxt_ref[units + begin : units + begin + 256]
+        dnormed2 = dnormed2 + mul(dswish, swish_t, nn_dims) + mul(dlinear, linear_t, nn_dims)
     dnormed2 = dnormed2.astype(bf16).astype(f32)
     dhat2 = dnormed2 * gain2
     dmiddle = rstd2 * (
@@ -442,8 +445,8 @@
         dhat_e - channel_sum(dhat_e) * inv_c - hat_e * (channel_sum(dhat_e * hat_e) * inv_c)
     )
     s3[...] = edge_raw.astype(bf16).astype(f32)
+    scatter(2, s3, r3, False)
     r3[me] = s3[me]
-    scatter(2, s3, r3, False)
 
     gate_grad = (late * update).astype(bf16).astype(f32)
     dgate = (gate_grad * gating * (1.0 - gating)).astype(bf16)
@@ -485,8 +488,8 @@
     s4[...] = jnp.concatenate(
         [left_grad.reshape(n, 8, 128), right_grad.reshape(n, 8, 128)], axis=1
     ).astype(bf16)
+    scatter(3, s4, r4, False)
     r4[me] = s4[me]
-    scatter(3, s4, r4, False)
     arrive(3, r4)
 
     grads = r4[...].astype(f32)
@@ -505,8 +508,8 @@
     s5[...] = jnp.concatenate(
         [gain1_sum, shift1_sum, gain2_sum, shift2_sum, gain_e_sum, shift_e_sum, blank], axis=0
     )
+    scatter(4, s5, r5, True)
     r5[me] = s5[...]
-    scatter(4, s5, r5, True)
     dhat1 = dnormed * gain1
     early = rstd1 * (
         dhat1
@@ -595,6 +598,7 @@
             pltpu.VMEM((8, 128), f32),
             tile,
             pltpu.VMEM((cells, w_contract.shape[0]), bf16),
+            pltpu.VMEM(w_expand.shape[::-1], bf16),
             pltpu.SemaphoreType.DMA((5,)),
             pltpu.SemaphoreType.DMA((5,)),
             pltpu.SemaphoreType.DMA((len(operands),)),

time: 30.6 us -> 30.8 us (level)
  no operation moved by 1% of the time
where the time goes in v4:
time: 30.8 us; the launch traced here: 30.7 us
  Pallas kernels  29.4 us (95%)
  between operations  1.29 us (4%)
    pallas_call x1, Pallas kernels, fused_body(): pl.pallas_call(functools.partial(fused_kernel, n), out_shape=(pltpu.VMEM(...  28.7 us
    pallas_call x1, Pallas kernels, fused_body(): pl.pallas_call(write_out, out_shape=tuple((jax.ShapeDtypeStruct(x.shape,...  0.66 us

profile of v4, /device:TPU:0, one launch (start us, length us, event | category | flops | bytes accessed | tf_op | source)
XLA Modules:
  0.0 30.7 jit_solution(15642882142806069344)
XLA Ops:
  1.3 28.7 %shard_map.166 = (bf16[4,64,128]{2,1,0:T(8,128)(2,1)S(1)}, f32[4,128]{1,0:T(4,128)S(1)}, f32[2,64]{1,0:T(2,128)S(1)}) custom-call(bf16[4,64,128]{2,1,0:T(8,128)(2,1)} %refs_0_.1, bf16[128,256]{1,0:T(8,128)(2,1)} %refs_1_.1, f32[1,128]{1,0:T(1,128)} %bitcast.8, f32[1,128]{1,0:T(1,128)} %bitcast.9, s32[4,64]{1,0:T(4,128)} %refs_4_.1, s32[1,1]{1,0:T(1,128)} %bitcast.7.refs_5_, ...), custom_call_target="tpu_custom_call" | custom-call | tf_op jit(solution)/shard_map/pallas_call | solution.py:579
  30.0 0.7 %shard_map.167 = (bf16[4,64,128]{2,1,0:T(8,128)(2,1)}, f32[4,128]{1,0:T(4,128)}, f32[2,64]{1,0:T(2,128)}) custom-call(bf16[4,64,128]{2,1,0:T(8,128)(2,1)S(1)} %get-tuple-element.6.a, f32[4,128]{1,0:T(4,128)S(1)} %get-tuple-element.7.b, f32[2,64]{1,0:T(2,128)S(1)} %get-tuple-element.8.c), custom_call_target="tpu_custom_call" | custom-call | tf_op jit(solution)/shard_map/pallas_call | solution.py:610
